TPU v7x, 32 devices: a whole 2x2x4 slice. The times are simulated.
32 devices in a mesh: gx: 8 (over y, x, core), gy: 4 (over z).
Axes of the slice: x: 2, y: 2, z: 4, core: 2. Of those that a mesh axis runs over, the one named last changes fastest.
Arguments:
- operator_blocks: float32 [16, 8, 12, 7, 64, 64], P('gx', 'gy'), may hold values from -1 to 13, as said below
- start_block: float32 [16, 8, 12, 64, 16], P('gx', 'gy'), may hold values from -4000 to 4000
Outputs:
- orthonormal: float32 [16, 8, 12, 64, 80], P('gx', 'gy')
- triangle: float32 [80, 80], replicated
Inputs may be any that keep to these rules, and one draw needn't show every extreme that they name: `operator_blocks`: the own block of every element is diagonally dominant; other entries are small.
All inputs are finite; a program needn't handle non-finite values.
Results may differ from a plain program's by a relative error of at most 0.0003.
Values sent between devices are 32-bit elements; how exact they have to be, the bound alone decides.
A program may use at most 64 MiB of HBM per device.

v0:
```python
import functools

import jax
import jax.numpy as jnp
from jax import lax
from jax.experimental import pallas as pl
from jax.experimental.pallas import tpu as pltpu
from jax.sharding import PartitionSpec as P

STEPS = 4
F32 = jnp.float32
BF16 = jnp.bfloat16
NT = (((1,), (1,)), ((), ()))
MESH = pl.DeviceIdType.MESH


def limbs(value):
    high = value.astype(BF16)
    return high, (value - high.astype(F32)).astype(BF16)


def dot_nt(left, right):
    return lax.dot_general(left, right, NT, preferred_element_type=F32)


def chunk_of(count, most):
    return max(size for size in range(1, most + 1) if count % size == 0)


def in_place_factor(blocks):
    width = 8 * len(blocks)
    lane = lax.broadcasted_iota(jnp.int32, blocks[0].shape, 1)
    rows = lax.broadcasted_iota(jnp.int32, blocks[0].shape, 0)
    blocks = list(blocks)
    for j in range(width):
        first, inside = divmod(j, 8)
        pivot_row = blocks[first][inside : inside + 1, :]
        inverse = 1.0 / pivot_row[:, j : j + 1]
        scaled = jnp.where(lane[:1] == j, 1.0, pivot_row) * inverse
        for b in range(first, len(blocks)):
            column = blocks[b][:, j : j + 1]
            kept = jnp.where(lane == j, 0.0, blocks[b])
            update = kept - column * scaled
            if b == first:
                update = jnp.where(rows > inside, update, blocks[b])
            blocks[b] = update
    return blocks


def kernel(dims, blocks_hbm, start_ref, ortho_hbm, tri_ref, raw, weights, tall, limb, vert,
           partial, rx, ry, gram_x, gram_y, ortho, raw_sem, ortho_sem, send_x, recv_x, send_y,
           recv_y, send_gx, recv_gx, send_gy, recv_gy):
    n_gx, n_gy, nx, ny, nz, unk, rhs = dims
    pairs = nz // 2
    wide = 2 * unk
    cols = (STEPS + 1) * rhs
    gx, gy = lax.axis_index("gx"), lax.axis_index("gy")
    columns = [(x, y) for x in range(nx) for y in range(ny)]
    chunk = chunk_of(pairs, 3)

    def raw_copy(c):
        x, y = columns[c]
        return pltpu.make_async_copy(blocks_hbm.at[x, y], raw.at[c], raw_sem.at[c])

    for c in range(len(columns)):
        raw_copy(c).start()

    barrier = pltpu.get_barrier_semaphore()
    for d in range(1, n_gx):
        pl.semaphore_signal(barrier, inc=1, device_id={"gx": lax.rem(gx + d, n_gx)}, device_id_type=MESH)
    for d in range(1, n_gy):
        pl.semaphore_signal(barrier, inc=1, device_id={"gy": lax.rem(gy + d, n_gy)}, device_id_type=MESH)

    def store_basis(k, c, m, value):
        x, y = columns[c]
        tall[k, x, y, m] = value
        high, low = limbs(value)
        limb[c, m, rhs * k : rhs * (k + 1)] = high
        limb[c, m, cols + rhs * k : cols + rhs * (k + 1)] = low
        if k < STEPS:
            both = jnp.concatenate([high, low], axis=0)
            vert[c, m, :, 0:unk] = both[:, 0:unk]
            vert[c, m + 2, :, unk:wide] = both[:, unk:wide]

    def borders(c):
        x, y = columns[c]
        return [("gx", 0, x == 0), ("gx", 1, x == nx - 1), ("gy", 0, y == 0), ("gy", 1, y == ny - 1)]

    def has(axis, side):
        here, count = (gx, n_gx) if axis == "gx" else (gy, n_gy)
        return here > 0 if side == 0 else here < count - 1

    def halo_copy(k, c, axis, side):
        x, y = columns[c]
        if axis == "gx":
            target, land, at, ss, rs = gx, rx, y, send_x, recv_x
        else:
            target, land, at, ss, rs = gy, ry, x, send_y, recv_y
        target = target - 1 if side == 0 else target + 1
        return pltpu.make_async_remote_copy(
            src_ref=tall.at[k, x, y], dst_ref=land.at[k, 1 - side, at],
            send_sem=ss.at[k, side, at], recv_sem=rs.at[k, 1 - side, at],
            device_id={axis: target}, device_id_type=MESH)

    def halo_wait(k, c, axis, side):
        x, y = columns[c]
        if axis == "gx":
            target, land, at, ss, rs = gx, rx, y, send_x, recv_x
        else:
            target, land, at, ss, rs = gy, ry, x, send_y, recv_y
        target = target - 1 if side == 0 else target + 1
        pltpu.make_async_remote_copy(
            src_ref=tall.at[k, x, y], dst_ref=land.at[k, side, at],
            send_sem=ss.at[k, side, at], recv_sem=rs.at[k, side, at],
            device_id={axis: target}, device_id_type=MESH).wait_recv()

    def send_column(k, c):
        for axis, side, edge in borders(c):
            if edge:
                @pl.when(has(axis, side))
                def _():
                    halo_copy(k, c, axis, side).start()

    for c, (x, y) in enumerate(columns):
        vert[c, 1, :, unk:wide] = jnp.zeros((2 * rhs, unk), BF16)
        vert[c, pairs, :, 0:unk] = jnp.zeros((2 * rhs, unk), BF16)
        for m in range(pairs):
            store_basis(0, c, m, jnp.concatenate([start_ref[x, y, 2 * m], start_ref[x, y, 2 * m + 1]], axis=1))
    for axis, land in (("gx", rx), ("gy", ry)):
        for side in (0, 1):
            @pl.when(jnp.logical_not(has(axis, side)))
            def _():
                for k in range(STEPS):
                    land[k, side] = jnp.zeros(land.shape[2:], F32)

    pl.semaphore_wait(barrier, n_gx + n_gy - 2)
    for c in range(len(columns)):
        send_column(0, c)

    def order(c):
        marks = [edge for _, _, edge in borders(c)]
        near = [d for d in range(4) if not marks[d]]
        far = [d for d in range(4) if marks[d]]
        return near, far

    zeros = jnp.zeros((unk, unk), F32)

    def prepare(c):
        near, far = order(c)

        def body(m, carry):
            low, up = raw.at[c, 2 * m], raw.at[c, 2 * m + 1]
            pieces = [
                ((low[0], low[6]), (up[5], up[0])),
                ((zeros, low[5]), (up[6], zeros)),
            ]
            for d in near + far:
                pieces.append(((low[1 + d], zeros), (zeros, up[1 + d])))
            for at, halves in enumerate(pieces):
                for half, (left, right) in enumerate(halves):
                    high, rest = limbs(jnp.concatenate([left, right], axis=1))
                    lanes = slice(at * wide, (at + 1) * wide)
                    weights[c, m, half * unk : (half + 1) * unk, lanes] = high
                    weights[c, m, wide + half * unk : wide + (half + 1) * unk, lanes] = rest
            return carry

        lax.fori_loop(0, pairs, body, 0)

    def fold(product):
        rows = product[0:rhs] + product[rhs : 2 * rhs]
        return rows[:, 0:wide] + rows[:, wide : 2 * wide]

    def rows_of(k, c, m):
        return jnp.concatenate(
            [limb[c, m, rhs * k : rhs * (k + 1)], limb[c, m, cols + rhs * k : cols + rhs * (k + 1)]], axis=0)

    def neighbour(c, d):
        x, y = columns[c]
        step = ((-1, 0), (1, 0), (0, -1), (0, 1))[d]
        return columns.index((x + step[0], y + step[1]))

    def near_part(k, c):
        near, _ = order(c)

        def body(i, carry):
            for s in range(chunk):
                m = i * chunk + s
                pieces = [rows_of(k, c, m), vert[c, m + 1]]
                pieces += [rows_of(k, neighbour(c, d), m) for d in near]
                left = jnp.concatenate(pieces, axis=1)
                partial[c, m] = fold(dot_nt(left, weights[c, m, :, 0 : left.shape[1]]))
            return carry

        lax.fori_loop(0, pairs // chunk, body, 0)

    def far_part(k, c):
        x, y = columns[c]
        near, far = order(c)
        for d in far:
            axis, side, _ = borders(c)[d]

            @pl.when(has(axis, side))
            def _():
                halo_wait(k, c, axis, side)

        def body(i, carry):
            for s in range(chunk):
                m = i * chunk + s
                pieces = []
                for d in far:
                    value = rx[k, d, y, m] if d < 2 else ry[k, d - 2, x, m]
                    pieces.append(jnp.concatenate(limbs(value), axis=0))
                applied = partial[c, m]
                if pieces:
                    left = jnp.concatenate(pieces, axis=1)
                    begin = (2 + len(near)) * wide
                    applied = applied + fold(dot_nt(left, weights[c, m, :, begin : begin + left.shape[1]]))
                current = tall[k, x, y, m]
                if k == 0:
                    following = (applied - 8.0 * current) * (1.0 / 6.0)
                else:
                    following = (applied - 8.0 * current) * (2.0 / 6.0) - tall[k - 1, x, y, m]
                store_basis(k + 1, c, m, following)
            return carry

        lax.fori_loop(0, pairs // chunk, body, 0)

    def gram_rows(k):
        count = rhs * (k + 1)
        total_high = jnp.zeros((2 * rhs, count), F32)
        total_low = jnp.zeros((2 * rhs, count), F32)
        for c in range(len(columns)):
            for m in range(0, pairs, 2):
                span = range(m, min(m + 2, pairs))
                left = jnp.concatenate([rows_of(k, c, q) for q in span], axis=1)
                high = jnp.concatenate([limb[c, q, 0:count] for q in span], axis=1)
                low = jnp.concatenate([limb[c, q, cols : cols + count] for q in span], axis=1)
                total_high += dot_nt(left, high)
                total_low += dot_nt(left, low)
        total = total_high + total_low
        gram_x[gx, rhs * k : rhs * (k + 1), 0:count] = total[0:rhs] + total[rhs : 2 * rhs]

    gram_x[gx] = jnp.zeros(gram_x.shape[1:], F32)
    for c in range(len(columns)):
        raw_copy(c).wait()
        prepare(c)
    for k in range(STEPS):
        for c in range(len(columns)):
            near_part(k, c)
        gram_rows(k)
        for c in range(len(columns)):
            far_part(k, c)
            if k + 1 < STEPS:
                send_column(k + 1, c)
    gram_rows(STEPS)

    def broadcast(axis, here, count, slots, send, recv):
        def copy(d):
            return pltpu.make_async_remote_copy(
                src_ref=slots.at[here], dst_ref=slots.at[here], send_sem=send.at[d], recv_sem=recv.at[here],
                device_id={axis: lax.rem(here + d, count)}, device_id_type=MESH)

        for d in range(1, count):
            copy(d).start()
        for d in range(1, count):
            source = lax.rem(here + d, count)
            pltpu.make_async_remote_copy(
                src_ref=slots.at[source], dst_ref=slots.at[source], send_sem=send.at[d], recv_sem=recv.at[source],
                device_id={axis: source}, device_id_type=MESH).wait_recv()
        total = slots[0]
        for i in range(1, count):
            total = total + slots[i]
        return total, copy

    total, copy_x = broadcast("gx", gx, n_gx, gram_x, send_gx, recv_gx)
    gram_y[gy] = total
    total, copy_y = broadcast("gy", gy, n_gy, gram_y, send_gy, recv_gy)

    rows = lax.broadcasted_iota(jnp.int32, (cols, wide), 0)
    lane = lax.broadcasted_iota(jnp.int32, (cols, wide), 1)
    square = jnp.concatenate([total, jnp.zeros((wide - cols, wide), F32)], axis=0)
    whole = jnp.where(lane > rows, square.T[0:cols], total)
    factored = in_place_factor([whole[8 * b : 8 * b + 8] for b in range(cols // 8)])
    factored = jnp.concatenate(factored, axis=0)
    diagonal = jnp.sum(jnp.where(lane == rows, factored, 0.0), axis=1, keepdims=True)
    root = jnp.sqrt(diagonal)
    scale = 1.0 / root
    upper = jnp.where(lane > rows, factored * scale, 0.0) + jnp.where(lane == rows, root, 0.0)
    tri_ref[...] = upper[:, 0:cols]
    inverse = (jnp.where(lane < rows, factored, 0.0) + jnp.where(lane == rows, 1.0, 0.0)) * scale
    inverse = jnp.concatenate([inverse, jnp.zeros((wide - cols, wide), F32)], axis=0)
    inverse_high, inverse_low = limbs(inverse)
    right = jnp.concatenate(
        [jnp.concatenate([inverse_high, inverse_high], axis=1), jnp.concatenate([inverse_low, inverse_low], axis=1)],
        axis=0)

    def ortho_copy(c):
        x, y = columns[c]
        return pltpu.make_async_copy(ortho.at[c], ortho_hbm.at[x, y], ortho_sem.at[c])

    for c, (x, y) in enumerate(columns):
        def body(i, carry):
            for s in range(chunk):
                m = i * chunk + s
                pieces = [tall[k, x, y, m] for k in range(STEPS + 1)]
                block = jnp.concatenate(pieces + [jnp.zeros((wide - cols, wide), F32)], axis=0).T
                product = dot_nt(jnp.concatenate(limbs(block), axis=1), right)
                result = (product[:, 0:wide] + product[:, wide : 2 * wide])[:, 0:cols]
                ortho[c, 2 * m] = result[0:unk]
                ortho[c, 2 * m + 1] = result[unk:wide]
            return carry

        lax.fori_loop(0, pairs // chunk, body, 0)
        ortho_copy(c).start()

    for d in range(1, n_gx):
        copy_x(d).wait_send()
    for d in range(1, n_gy):
        copy_y(d).wait_send()
    for k in range(STEPS):
        for c in range(len(columns)):
            for axis, side, edge in borders(c):
                if edge:
                    @pl.when(has(axis, side))
                    def _():
                        halo_copy(k, c, axis, side).wait_send()
    for c in range(len(columns)):
        ortho_copy(c).wait()


def per_device(operator_blocks, start_block):
    nx, ny, nz, _, unk, _ = operator_blocks.shape
    rhs = start_block.shape[-1]
    n_gx, n_gy = lax.axis_size("gx"), lax.axis_size("gy")
    pairs, wide, cols, count = nz // 2, 2 * unk, (STEPS + 1) * rhs, nx * ny
    assert nz % 2 == 0 and wide == 128 and rhs % 16 == 0 and cols <= wide
    dma = pltpu.SemaphoreType.DMA
    return pl.pallas_call(
        functools.partial(kernel, (n_gx, n_gy, nx, ny, nz, unk, rhs)),
        out_shape=(
            jax.ShapeDtypeStruct((nx, ny, nz, unk, cols), F32),
            jax.ShapeDtypeStruct((cols, cols), F32),
        ),
        in_specs=[pl.BlockSpec(memory_space=pl.ANY), pl.BlockSpec(memory_space=pltpu.VMEM)],
        out_specs=(pl.BlockSpec(memory_space=pl.ANY), pl.BlockSpec(memory_space=pltpu.VMEM)),
        scratch_shapes=[
            pltpu.VMEM((count, nz, 7, unk, unk), F32),
            pltpu.VMEM((count, pairs, 2 * wide, 6 * wide), BF16),
            pltpu.VMEM((STEPS + 1, nx, ny, pairs, rhs, wide), F32),
            pltpu.VMEM((count, pairs, 2 * cols, wide), BF16),
            pltpu.VMEM((count, pairs + 2, 2 * rhs, wide), BF16),
            pltpu.VMEM((count, pairs, rhs, wide), F32),
            pltpu.VMEM((STEPS, 2, ny, pairs, rhs, wide), F32),
            pltpu.VMEM((STEPS, 2, nx, pairs, rhs, wide), F32),
            pltpu.VMEM((n_gx, cols, wide), F32),
            pltpu.VMEM((n_gy, cols, wide), F32),
            pltpu.VMEM((count, nz, unk, cols), F32),
            dma((count,)),
            dma((count,)),
            dma((STEPS, 2, ny)),
            dma((STEPS, 2, ny)),
            dma((STEPS, 2, nx)),
            dma((STEPS, 2, nx)),
            dma((n_gx,)),
            dma((n_gx,)),
            dma((n_gy,)),
            dma((n_gy,)),
        ],
        compiler_params=pltpu.CompilerParams(
            collective_id=0, has_side_effects=True, vmem_limit_bytes=52 * 1024 * 1024
        ),
        cost_estimate=pl.CostEstimate(flops=6_000_000_000, bytes_accessed=16_000_000, transcendentals=0),
    )(operator_blocks, jnp.swapaxes(start_block, -1, -2))


def solution(mesh):
    in_specs = (P("gx", "gy", None, None, None, None), P("gx", "gy", None, None, None))
    out_specs = (P("gx", "gy", None, None, None), P())
    return jax.shard_map(
        per_device, mesh=mesh, in_specs=in_specs, out_specs=out_specs, check_vma=False
    )
```

profile of v0, /device:TPU:0, one launch (start us, length us, event | category | flops | bytes accessed | tf_op | source)
XLA Modules:
  0.0 53.5 jit_solution(15277999485551304510)
XLA Ops:
  0.6 0.0 copy-start
  0.6 1.0 %copy-done = f32[2,2,12,64,16]{3,4,2,1,0:T(8,128)S(1)} copy-done((f32[2,2,12,64,16]{3,4,2,1,0:T(8,128)S(1)}, f32[2,2,12,64,16]{3,4,2,1,0:T(8,128)}, u32[]{:S(2)}) %copy-start) | copy-done | bytes 196632
  1.6 50.1 %shard_map.41 = (f32[2,2,12,64,80]{4,3,2,1,0:T(8,128)S(1)}, f32[80,80]{1,0:T(8,128)S(1)}) custom-call(f32[2,2,12,7,64,64]{5,4,3,2,1,0:T(8,128)} %blocks_hbm.1, f32[2,2,12,16,64]{4,3,2,1,0:T(8,128)S(1)} %bitcast.1), custom_call_target="tpu_custom_call" | custom-call | flops 6000000000 | bytes 16000000 | tf_op jit(solution)/shard_map/pallas_call | solution.py:338
  51.7 1.1 %copy.6 = f32[2,2,12,64,80]{4,3,2,1,0:T(8,128)} copy(f32[2,2,12,64,80]{4,3,2,1,0:T(8,128)S(1)} %get-tuple-element.4) | data formatting | bytes 1966080
  52.9 0.6 %copy.7 = f32[80,80]{1,0:T(8,128)} copy(f32[80,80]{1,0:T(8,128)S(1)} %get-tuple-element.5) | data formatting | bytes 51200
Async XLA Ops:
  0.6 1.0 %copy-start = (f32[2,2,12,64,16]{3,4,2,1,0:T(8,128)S(1)}, f32[2,2,12,64,16]{3,4,2,1,0:T(8,128)}, u32[]{:S(2)}) copy-start(f32[2,2,12,64,16]{3,4,2,1,0:T(8,128)} %param.3) | copy-start | bytes 589828
where the time goes:
time: 53.6 us; the launch traced here: 53.5 us
  Pallas kernels  50.1 us (93%)
  local copies, waits for them, and re-layouts  2.75 us (5%)
  between operations  0.65 us (1%)
    pallas_call x1, Pallas kernels, per_device(): pl.pallas_call(functools.partial(kernel, (n_gx, n_gy, nx, ny, nz, unk, rh...  50.1 us
    unnamed x4, local copies, waits for them, and re-layouts  2.75 us

commit v1 on v0

--- a/solution.py
+++ b/solution.py
@@ -27,29 +27,53 @@
     return max(size for size in range(1, most + 1) if count % size == 0)
 
 
-def in_place_factor(blocks):
-    width = 8 * len(blocks)
+def dot_full(left, right, dims=(((1,), (0,)), ((), ()))):
+    return lax.dot_general(left, right, dims, precision=lax.Precision.HIGHEST, preferred_element_type=F32)
+
+
+def eliminate(blocks, start, stop):
     lane = lax.broadcasted_iota(jnp.int32, blocks[0].shape, 1)
     rows = lax.broadcasted_iota(jnp.int32, blocks[0].shape, 0)
+    line = lane[:1]
     blocks = list(blocks)
-    for j in range(width):
+    for j in range(start, stop, 2):
         first, inside = divmod(j, 8)
-        pivot_row = blocks[first][inside : inside + 1, :]
-        inverse = 1.0 / pivot_row[:, j : j + 1]
-        scaled = jnp.where(lane[:1] == j, 1.0, pivot_row) * inverse
-        for b in range(first, len(blocks)):
-            column = blocks[b][:, j : j + 1]
-            kept = jnp.where(lane == j, 0.0, blocks[b])
-            update = kept - column * scaled
-            if b == first:
-                update = jnp.where(rows > inside, update, blocks[b])
-            blocks[b] = update
+        row_0 = blocks[first][inside : inside + 1, :]
+        row_1 = blocks[first][inside + 1 : inside + 2, :]
+        a, b, c = row_0[:, j : j + 1], row_0[:, j + 1 : j + 2], row_1[:, j + 1 : j + 2]
+        inverse = 1.0 / (a * c - b * b)
+        unit_0 = jnp.where(line == j, 1.0, jnp.where(line == j + 1, 0.0, row_0))
+        unit_1 = jnp.where(line == j + 1, 1.0, jnp.where(line == j, 0.0, row_1))
+        scaled_0 = (c * unit_0 - b * unit_1) * inverse
+        scaled_1 = (a * unit_1 - b * unit_0) * inverse
+        ratio = b / a
+        second = jnp.where(line == j, -ratio, row_1 - ratio * row_0)
+        pair = jnp.logical_or(lane == j, lane == j + 1)
+        for i in range(first, len(blocks)):
+            block = blocks[i]
+            kept = jnp.where(pair, 0.0, block)
+            update = kept - block[:, j : j + 1] * scaled_0 - block[:, j + 1 : j + 2] * scaled_1
+            if i == first:
+                update = jnp.where(rows > inside + 1, update, jnp.where(rows == inside + 1, second, block))
+            blocks[i] = update
     return blocks
 
 
-def kernel(dims, blocks_hbm, start_ref, ortho_hbm, tri_ref, raw, weights, tall, limb, vert,
-           partial, rx, ry, gram_x, gram_y, ortho, raw_sem, ortho_sem, send_x, recv_x, send_y,
-           recv_y, send_gx, recv_gx, send_gy, recv_gy):
+def split_factor(blocks):
+    factored = jnp.concatenate(blocks, axis=0)
+    lane = lax.broadcasted_iota(jnp.int32, factored.shape, 1)
+    rows = lax.broadcasted_iota(jnp.int32, factored.shape, 0)
+    diagonal = jnp.sum(jnp.where(lane == rows, factored, 0.0), axis=1, keepdims=True)
+    root = jnp.sqrt(diagonal)
+    scale = 1.0 / root
+    upper = jnp.where(lane > rows, factored * scale, jnp.where(lane == rows, root, 0.0))
+    inverse = jnp.where(lane < rows, factored * scale, jnp.where(lane == rows, scale, 0.0))
+    return upper, inverse
+
+
+def kernel(dims, blocks_hbm, start_hbm, ortho_hbm, tri_ref, start_ref, raw, weights, tall, limb, vert,
+           partial, rx, ry, gram_x, gram_y, turned, ortho, start_sem, raw_sem, ortho_sem, send_x, recv_x,
+           send_y, recv_y, send_gx, recv_gx, send_gy, recv_gy):
     n_gx, n_gy, nx, ny, nz, unk, rhs = dims
     pairs = nz // 2
     wide = 2 * unk
@@ -62,6 +86,8 @@
         x, y = columns[c]
         return pltpu.make_async_copy(blocks_hbm.at[x, y], raw.at[c], raw_sem.at[c])
 
+    start_copy = pltpu.make_async_copy(start_hbm, start_ref, start_sem)
+    start_copy.start()
     for c in range(len(columns)):
         raw_copy(c).start()
 
@@ -121,6 +147,7 @@
                 def _():
                     halo_copy(k, c, axis, side).start()
 
+    start_copy.wait()
     for c, (x, y) in enumerate(columns):
         vert[c, 1, :, unk:wide] = jnp.zeros((2 * rhs, unk), BF16)
         vert[c, pairs, :, 0:unk] = jnp.zeros((2 * rhs, unk), BF16)
@@ -238,57 +265,105 @@
                 total_high += dot_nt(left, high)
                 total_low += dot_nt(left, low)
         total = total_high + total_low
-        gram_x[gx, rhs * k : rhs * (k + 1), 0:count] = total[0:rhs] + total[rhs : 2 * rhs]
-
-    gram_x[gx] = jnp.zeros(gram_x.shape[1:], F32)
+        total = total[0:rhs] + total[rhs : 2 * rhs]
+        gram_x[k, gx] = jnp.concatenate([total, jnp.zeros((rhs, wide - count), F32)], axis=1)
+
     for c in range(len(columns)):
         raw_copy(c).wait()
         prepare(c)
+    axes = {"gx": (gx, n_gx, gram_x, send_gx, recv_gx), "gy": (gy, n_gy, gram_y, send_gy, recv_gy)}
+
+    def gram_copy(axis, k, d, receive=False):
+        here, count, slots, send, recv = axes[axis]
+        other = lax.rem(here + d, count)
+        slot = other if receive else here
+        return pltpu.make_async_remote_copy(
+            src_ref=slots.at[k, slot], dst_ref=slots.at[k, slot], send_sem=send.at[k, d],
+            recv_sem=recv.at[k, slot], device_id={axis: other}, device_id_type=MESH)
+
+    def gram_send(axis, k):
+        for d in range(1, axes[axis][1]):
+            gram_copy(axis, k, d).start()
+
+    def gram_sum(axis, k):
+        _, count, slots, _, _ = axes[axis]
+        for d in range(1, count):
+            gram_copy(axis, k, d, receive=True).wait_recv()
+        total = slots[k, 0]
+        for i in range(1, count):
+            total = total + slots[k, i]
+        return total
+
+    def gram_turn(k):
+        gram_y[k, gy] = gram_sum("gx", k)
+        gram_send("gy", k)
+
     for k in range(STEPS):
+        gram_rows(k)
+        gram_send("gx", k)
         for c in range(len(columns)):
             near_part(k, c)
-        gram_rows(k)
+        gram_turn(k)
         for c in range(len(columns)):
             far_part(k, c)
             if k + 1 < STEPS:
                 send_column(k + 1, c)
     gram_rows(STEPS)
-
-    def broadcast(axis, here, count, slots, send, recv):
-        def copy(d):
-            return pltpu.make_async_remote_copy(
-                src_ref=slots.at[here], dst_ref=slots.at[here], send_sem=send.at[d], recv_sem=recv.at[here],
-                device_id={axis: lax.rem(here + d, count)}, device_id_type=MESH)
-
-        for d in range(1, count):
-            copy(d).start()
-        for d in range(1, count):
-            source = lax.rem(here + d, count)
-            pltpu.make_async_remote_copy(
-                src_ref=slots.at[source], dst_ref=slots.at[source], send_sem=send.at[d], recv_sem=recv.at[source],
-                device_id={axis: source}, device_id_type=MESH).wait_recv()
-        total = slots[0]
-        for i in range(1, count):
-            total = total + slots[i]
-        return total, copy
-
-    total, copy_x = broadcast("gx", gx, n_gx, gram_x, send_gx, recv_gx)
-    gram_y[gy] = total
-    total, copy_y = broadcast("gy", gy, n_gy, gram_y, send_gy, recv_gy)
-
-    rows = lax.broadcasted_iota(jnp.int32, (cols, wide), 0)
-    lane = lax.broadcasted_iota(jnp.int32, (cols, wide), 1)
-    square = jnp.concatenate([total, jnp.zeros((wide - cols, wide), F32)], axis=0)
-    whole = jnp.where(lane > rows, square.T[0:cols], total)
-    factored = in_place_factor([whole[8 * b : 8 * b + 8] for b in range(cols // 8)])
-    factored = jnp.concatenate(factored, axis=0)
-    diagonal = jnp.sum(jnp.where(lane == rows, factored, 0.0), axis=1, keepdims=True)
-    root = jnp.sqrt(diagonal)
-    scale = 1.0 / root
-    upper = jnp.where(lane > rows, factored * scale, 0.0) + jnp.where(lane == rows, root, 0.0)
-    tri_ref[...] = upper[:, 0:cols]
-    inverse = (jnp.where(lane < rows, factored, 0.0) + jnp.where(lane == rows, 1.0, 0.0)) * scale
-    inverse = jnp.concatenate([inverse, jnp.zeros((wide - cols, wide), F32)], axis=0)
+    gram_send("gx", STEPS)
+
+    for c, (x, y) in enumerate(columns):
+        def turn(i, carry):
+            for s in range(chunk):
+                m = i * chunk + s
+                pieces = [tall[k, x, y, m] for k in range(STEPS + 1)]
+                block = jnp.concatenate(pieces + [jnp.zeros((wide - cols, wide), F32)], axis=0).T
+                turned[c, m] = jnp.concatenate(limbs(block), axis=1)
+            return carry
+
+        lax.fori_loop(0, pairs // chunk, turn, 0)
+
+    front = STEPS * rhs
+    rows = lax.broadcasted_iota(jnp.int32, (front, wide), 0)
+    lane = lax.broadcasted_iota(jnp.int32, (front, wide), 1)
+    lower = jnp.concatenate([gram_sum("gy", k) for k in range(STEPS)], axis=0)
+    square = jnp.concatenate([lower, jnp.zeros((wide - front, wide), F32)], axis=0)
+    whole = jnp.where(lane > rows, square.T[0:front], lower)
+    on_diagonal = jnp.where(lane == rows, whole, 0.0)
+    norm_rows = jnp.sqrt(jnp.sum(on_diagonal, axis=1, keepdims=True))
+    norm_front = jnp.sqrt(jnp.sum(on_diagonal, axis=0, keepdims=True))
+    line = lane[:1]
+    whole = whole / (norm_rows * jnp.where(line < front, norm_front, 1.0))
+    factored = [whole[8 * i : 8 * i + 8] for i in range(front // 8)]
+    factored = eliminate(factored, 0, rhs)
+    gram_turn(STEPS)
+    factored = eliminate(factored, rhs, front)
+    upper, inverse = split_factor(factored)
+    inverse_full = jnp.concatenate([inverse, jnp.zeros((wide - front, wide), F32)], axis=0)
+
+    last = gram_sum("gy", STEPS)
+    last_rows = lax.broadcasted_iota(jnp.int32, (rhs, wide), 0)
+    last_lane = lax.broadcasted_iota(jnp.int32, (rhs, wide), 1)
+    on_diagonal = jnp.where(last_lane == last_rows + front, last, 0.0)
+    norm_rows = jnp.sqrt(jnp.sum(on_diagonal, axis=1, keepdims=True))
+    norm = norm_front + jnp.sqrt(jnp.sum(on_diagonal, axis=0, keepdims=True))
+    norm = jnp.where(line < cols, norm, 1.0)
+    last = last / (norm_rows * norm)
+    side = dot_full(jnp.where(last_lane < front, last, 0.0), inverse_full, NT)
+    rest = last[:, front:cols] - dot_full(side, side, NT)
+    rest = jnp.concatenate([rest, jnp.zeros((rhs, wide - rhs), F32)], axis=1)
+    rest = eliminate([rest[8 * i : 8 * i + 8] for i in range(rhs // 8)], 0, rhs)
+    rest_upper, rest_inverse = split_factor(rest)
+    below = dot_full(rest_inverse[:, 0:rhs], dot_full(side, inverse_full))
+
+    def placed(value):
+        return jnp.concatenate(
+            [jnp.zeros((rhs, front), F32), value[:, 0:rhs], jnp.zeros((rhs, wide - cols), F32)], axis=1)
+
+    beside = jnp.concatenate([jnp.zeros((front, wide), F32), side, jnp.zeros((wide - cols, wide), F32)], axis=0)
+    triangle = jnp.concatenate([upper + beside.T[0:front], placed(rest_upper)], axis=0) * norm
+    tri_ref[...] = triangle[:, 0:cols]
+    inverse = jnp.concatenate(
+        [inverse, placed(rest_inverse) - below, jnp.zeros((wide - cols, wide), F32)], axis=0) / norm
     inverse_high, inverse_low = limbs(inverse)
     right = jnp.concatenate(
         [jnp.concatenate([inverse_high, inverse_high], axis=1), jnp.concatenate([inverse_low, inverse_low], axis=1)],
@@ -302,9 +377,7 @@
         def body(i, carry):
             for s in range(chunk):
                 m = i * chunk + s
-                pieces = [tall[k, x, y, m] for k in range(STEPS + 1)]
-                block = jnp.concatenate(pieces + [jnp.zeros((wide - cols, wide), F32)], axis=0).T
-                product = dot_nt(jnp.concatenate(limbs(block), axis=1), right)
+                product = dot_nt(turned[c, m], right)
                 result = (product[:, 0:wide] + product[:, wide : 2 * wide])[:, 0:cols]
                 ortho[c, 2 * m] = result[0:unk]
                 ortho[c, 2 * m + 1] = result[unk:wide]
@@ -313,10 +386,10 @@
         lax.fori_loop(0, pairs // chunk, body, 0)
         ortho_copy(c).start()
 
-    for d in range(1, n_gx):
-        copy_x(d).wait_send()
-    for d in range(1, n_gy):
-        copy_y(d).wait_send()
+    for k in range(STEPS + 1):
+        for axis in axes:
+            for d in range(1, axes[axis][1]):
+                gram_copy(axis, k, d).wait_send()
     for k in range(STEPS):
         for c in range(len(columns)):
             for axis, side, edge in borders(c):
@@ -341,9 +414,10 @@
             jax.ShapeDtypeStruct((nx, ny, nz, unk, cols), F32),
             jax.ShapeDtypeStruct((cols, cols), F32),
         ),
-        in_specs=[pl.BlockSpec(memory_space=pl.ANY), pl.BlockSpec(memory_space=pltpu.VMEM)],
+        in_specs=[pl.BlockSpec(memory_space=pl.ANY), pl.BlockSpec(memory_space=pl.ANY)],
         out_specs=(pl.BlockSpec(memory_space=pl.ANY), pl.BlockSpec(memory_space=pltpu.VMEM)),
         scratch_shapes=[
+            pltpu.VMEM((nx, ny, nz, rhs, unk), F32),
             pltpu.VMEM((count, nz, 7, unk, unk), F32),
             pltpu.VMEM((count, pairs, 2 * wide, 6 * wide), BF16),
             pltpu.VMEM((STEPS + 1, nx, ny, pairs, rhs, wide), F32),
@@ -352,19 +426,21 @@
             pltpu.VMEM((count, pairs, rhs, wide), F32),
             pltpu.VMEM((STEPS, 2, ny, pairs, rhs, wide), F32),
             pltpu.VMEM((STEPS, 2, nx, pairs, rhs, wide), F32),
-            pltpu.VMEM((n_gx, cols, wide), F32),
-            pltpu.VMEM((n_gy, cols, wide), F32),
+            pltpu.VMEM((STEPS + 1, n_gx, rhs, wide), F32),
+            pltpu.VMEM((STEPS + 1, n_gy, rhs, wide), F32),
+            pltpu.VMEM((count, pairs, wide, 2 * wide), BF16),
             pltpu.VMEM((count, nz, unk, cols), F32),
+            dma,
             dma((count,)),
             dma((count,)),
             dma((STEPS, 2, ny)),
             dma((STEPS, 2, ny)),
             dma((STEPS, 2, nx)),
             dma((STEPS, 2, nx)),
-            dma((n_gx,)),
-            dma((n_gx,)),
-            dma((n_gy,)),
-            dma((n_gy,)),
+            dma((STEPS + 1, n_gx)),
+            dma((STEPS + 1, n_gx)),
+            dma((STEPS + 1, n_gy)),
+            dma((STEPS + 1, n_gy)),
         ],
         compiler_params=pltpu.CompilerParams(
             collective_id=0, has_side_effects=True, vmem_limit_bytes=52 * 1024 * 1024

time: 53.6 us -> 54.1 us (level)
  no operation moved by 1% of the time
where the time goes in v1:
time: 54.1 us; the launch traced here: 54 us
  Pallas kernels  50.6 us (94%)
  local copies, waits for them, and re-layouts  2.75 us (5%)
  between operations  0.65 us (1%)
    pallas_call x1, Pallas kernels, per_device(): pl.pallas_call(functools.partial(kernel, (n_gx, n_gy, nx, ny, nz, unk, rh...  50.6 us
    unnamed x4, local copies, waits for them, and re-layouts  2.75 us

profile of v1, /device:TPU:0, one launch (start us, length us, event | category | flops | bytes accessed | tf_op | source)
XLA Modules:
  0.0 54.0 jit_solution(3904204759122729270)
XLA Ops:
  0.6 0.0 copy-start
  0.6 1.0 %copy-done = f32[2,2,12,64,16]{3,4,2,1,0:T(8,128)S(1)} copy-done((f32[2,2,12,64,16]{3,4,2,1,0:T(8,128)S(1)}, f32[2,2,12,64,16]{3,4,2,1,0:T(8,128)}, u32[]{:S(2)}) %copy-start) | copy-done | bytes 196632
  1.6 50.6 %shard_map.41 = (f32[2,2,12,64,80]{4,3,2,1,0:T(8,128)S(1)}, f32[80,80]{1,0:T(8,128)S(1)}) custom-call(f32[2,2,12,7,64,64]{5,4,3,2,1,0:T(8,128)} %blocks_hbm.1, f32[2,2,12,16,64]{4,3,2,1,0:T(8,128)S(1)} %bitcast.1), custom_call_target="tpu_custom_call" | custom-call | flops 6000000000 | bytes 16000000 | tf_op jit(solution)/shard_map/pallas_call | solution.py:411
  52.2 1.1 %copy.6 = f32[2,2,12,64,80]{4,3,2,1,0:T(8,128)} copy(f32[2,2,12,64,80]{4,3,2,1,0:T(8,128)S(1)} %get-tuple-element.4) | data formatting | bytes 1966080
  53.4 0.6 %copy.7 = f32[80,80]{1,0:T(8,128)} copy(f32[80,80]{1,0:T(8,128)S(1)} %get-tuple-element.5) | data formatting | bytes 51200
Async XLA Ops:
  0.6 1.0 %copy-start = (f32[2,2,12,64,16]{3,4,2,1,0:T(8,128)S(1)}, f32[2,2,12,64,16]{3,4,2,1,0:T(8,128)}, u32[]{:S(2)}) copy-start(f32[2,2,12,64,16]{3,4,2,1,0:T(8,128)} %param.3) | copy-start | bytes 589828

commit v2 on v1

--- a/solution.py
+++ b/solution.py
@@ -71,25 +71,67 @@
     return upper, inverse
 
 
-def kernel(dims, blocks_hbm, start_hbm, ortho_hbm, tri_ref, start_ref, raw, weights, tall, limb, vert,
-           partial, rx, ry, gram_x, gram_y, turned, ortho, start_sem, raw_sem, ortho_sem, send_x, recv_x,
-           send_y, recv_y, send_gx, recv_gx, send_gy, recv_gy):
+class Columns:
+    def __init__(self, nx, ny):
+        self.at = [(x, y) for x in range(nx) for y in range(ny)]
+        self.nx, self.ny = nx, ny
+
+    def borders(self, c):
+        x, y = self.at[c]
+        return [("gx", 0, x == 0), ("gx", 1, x == self.nx - 1), ("gy", 0, y == 0), ("gy", 1, y == self.ny - 1)]
+
+    def order(self, c):
+        marks = [edge for _, _, edge in self.borders(c)]
+        return sorted(range(4), key=lambda d: marks[d])
+
+    def neighbour(self, c, d):
+        x, y = self.at[c]
+        x, y = x + (-1, 1, 0, 0)[d], y + (0, 0, -1, 1)[d]
+        return self.at.index((x, y)) if (x, y) in self.at else None
+
+
+def repack_kernel(dims, blocks_hbm, weights, raw, raw_sem):
+    nx, ny, nz, unk, rhs = dims
+    columns = Columns(nx, ny)
+    wide = 2 * unk
+
+    def raw_copy(c):
+        x, y = columns.at[c]
+        return pltpu.make_async_copy(blocks_hbm.at[x, y], raw.at[c], raw_sem.at[c])
+
+    for c in range(len(columns.at)):
+        raw_copy(c).start()
+    for c in range(len(columns.at)):
+        raw_copy(c).wait()
+        first, second, third, fourth = (1 + d for d in columns.order(c))
+        zeros = jnp.zeros((unk, unk), F32)
+
+        def body(m, carry):
+            low, up = raw.at[c, 2 * m], raw.at[c, 2 * m + 1]
+            halves = (
+                ((low[0], low[6]), (low[first], low[5]), (low[third], low[fourth]), (low[second], zeros)),
+                ((up[5], up[0]), (up[6], up[first]), (up[fourth], up[third]), (zeros, up[second])),
+            )
+            for half, pieces in enumerate(halves):
+                for at, (left, right) in enumerate(pieces):
+                    high, rest = limbs(jnp.concatenate([left, right], axis=1))
+                    lanes = slice(at * wide, (at + 1) * wide)
+                    weights[c, m, half, 0:unk, lanes] = high
+                    weights[c, m, half, unk : 2 * unk, lanes] = rest
+            return carry
+
+        lax.fori_loop(0, nz // 2, body, 0)
+
+def steps_kernel(dims, weights, start_ref, turned, gram_ref, tall, limb, mixed, partial, rx, ry, gram_x, gram_y,
+                 send_x, recv_x, send_y, recv_y, send_gx, recv_gx, send_gy, recv_gy):
     n_gx, n_gy, nx, ny, nz, unk, rhs = dims
     pairs = nz // 2
     wide = 2 * unk
     cols = (STEPS + 1) * rhs
     gx, gy = lax.axis_index("gx"), lax.axis_index("gy")
-    columns = [(x, y) for x in range(nx) for y in range(ny)]
-    chunk = chunk_of(pairs, 3)
-
-    def raw_copy(c):
-        x, y = columns[c]
-        return pltpu.make_async_copy(blocks_hbm.at[x, y], raw.at[c], raw_sem.at[c])
-
-    start_copy = pltpu.make_async_copy(start_hbm, start_ref, start_sem)
-    start_copy.start()
-    for c in range(len(columns)):
-        raw_copy(c).start()
+    geometry = Columns(nx, ny)
+    columns, borders, order, neighbour = geometry.at, geometry.borders, geometry.order, geometry.neighbour
+    chunk = chunk_of(pairs, 6)
 
     barrier = pltpu.get_barrier_semaphore()
     for d in range(1, n_gx):
@@ -105,12 +147,12 @@
         limb[c, m, cols + rhs * k : cols + rhs * (k + 1)] = low
         if k < STEPS:
             both = jnp.concatenate([high, low], axis=0)
-            vert[c, m, :, 0:unk] = both[:, 0:unk]
-            vert[c, m + 2, :, unk:wide] = both[:, unk:wide]
-
-    def borders(c):
-        x, y = columns[c]
-        return [("gx", 0, x == 0), ("gx", 1, x == nx - 1), ("gy", 0, y == 0), ("gy", 1, y == ny - 1)]
+            mixed[c, m, 1, :, 0:unk] = both[:, 0:unk]
+            mixed[c, m + 2, 0, :, unk:wide] = both[:, unk:wide]
+            for user in range(len(columns)):
+                if neighbour(user, order(user)[0]) == c:
+                    mixed[user, m + 1, 0, :, 0:unk] = both[:, 0:unk]
+                    mixed[user, m + 1, 1, :, unk:wide] = both[:, unk:wide]
 
     def has(axis, side):
         here, count = (gx, n_gx) if axis == "gx" else (gy, n_gy)
@@ -147,10 +189,9 @@
                 def _():
                     halo_copy(k, c, axis, side).start()
 
-    start_copy.wait()
     for c, (x, y) in enumerate(columns):
-        vert[c, 1, :, unk:wide] = jnp.zeros((2 * rhs, unk), BF16)
-        vert[c, pairs, :, 0:unk] = jnp.zeros((2 * rhs, unk), BF16)
+        mixed[c, 1, 0, :, unk:wide] = jnp.zeros((2 * rhs, unk), BF16)
+        mixed[c, pairs, 1, :, 0:unk] = jnp.zeros((2 * rhs, unk), BF16)
         for m in range(pairs):
             store_basis(0, c, m, jnp.concatenate([start_ref[x, y, 2 * m], start_ref[x, y, 2 * m + 1]], axis=1))
     for axis, land in (("gx", rx), ("gy", ry)):
@@ -164,84 +205,60 @@
     for c in range(len(columns)):
         send_column(0, c)
 
-    def order(c):
-        marks = [edge for _, _, edge in borders(c)]
-        near = [d for d in range(4) if not marks[d]]
-        far = [d for d in range(4) if marks[d]]
-        return near, far
-
-    zeros = jnp.zeros((unk, unk), F32)
-
-    def prepare(c):
-        near, far = order(c)
-
-        def body(m, carry):
-            low, up = raw.at[c, 2 * m], raw.at[c, 2 * m + 1]
-            pieces = [
-                ((low[0], low[6]), (up[5], up[0])),
-                ((zeros, low[5]), (up[6], zeros)),
-            ]
-            for d in near + far:
-                pieces.append(((low[1 + d], zeros), (zeros, up[1 + d])))
-            for at, halves in enumerate(pieces):
-                for half, (left, right) in enumerate(halves):
-                    high, rest = limbs(jnp.concatenate([left, right], axis=1))
-                    lanes = slice(at * wide, (at + 1) * wide)
-                    weights[c, m, half * unk : (half + 1) * unk, lanes] = high
-                    weights[c, m, wide + half * unk : wide + (half + 1) * unk, lanes] = rest
-            return carry
-
-        lax.fori_loop(0, pairs, body, 0)
-
-    def fold(product):
-        rows = product[0:rhs] + product[rhs : 2 * rhs]
-        return rows[:, 0:wide] + rows[:, wide : 2 * wide]
+    def apply_tile(c, m, tile, operands):
+        results = []
+        for half in range(2):
+            product = dot_nt(weights[c, m, half, :, 2 * wide * tile : 2 * wide * (tile + 1)], operands[half])
+            results.append(product[0:unk] + product[unk : 2 * unk])
+        return jnp.concatenate(results, axis=0)
 
     def rows_of(k, c, m):
         return jnp.concatenate(
             [limb[c, m, rhs * k : rhs * (k + 1)], limb[c, m, cols + rhs * k : cols + rhs * (k + 1)]], axis=0)
 
-    def neighbour(c, d):
-        x, y = columns[c]
-        step = ((-1, 0), (1, 0), (0, -1), (0, 1))[d]
-        return columns.index((x + step[0], y + step[1]))
+    def wait_halos(k, c):
+        for axis, side, edge in borders(c):
+            if edge:
+                @pl.when(has(axis, side))
+                def _():
+                    halo_wait(k, c, axis, side)
 
     def near_part(k, c):
-        near, _ = order(c)
-
         def body(i, carry):
             for s in range(chunk):
                 m = i * chunk + s
-                pieces = [rows_of(k, c, m), vert[c, m + 1]]
-                pieces += [rows_of(k, neighbour(c, d), m) for d in near]
-                left = jnp.concatenate(pieces, axis=1)
-                partial[c, m] = fold(dot_nt(left, weights[c, m, :, 0 : left.shape[1]]))
+                own = rows_of(k, c, m)
+                operands = [jnp.concatenate([own, mixed[c, m + 1, half]], axis=1) for half in range(2)]
+                partial[c, m] = apply_tile(c, m, 0, operands)
             return carry
 
         lax.fori_loop(0, pairs // chunk, body, 0)
 
     def far_part(k, c):
         x, y = columns[c]
-        near, far = order(c)
-        for d in far:
-            axis, side, _ = borders(c)[d]
-
-            @pl.when(has(axis, side))
-            def _():
-                halo_wait(k, c, axis, side)
+        _, second, third, fourth = order(c)
+        wait_halos(k, c)
+
+        def values(d, m):
+            other = neighbour(c, d)
+            if other is None:
+                return rx[k, d, y, m] if d < 2 else ry[k, d - 2, x, m]
+            return tall[k, columns[other][0], columns[other][1], m]
 
         def body(i, carry):
+            in_low = lax.broadcasted_iota(jnp.int32, (rhs, wide), 1) < unk
             for s in range(chunk):
                 m = i * chunk + s
-                pieces = []
-                for d in far:
-                    value = rx[k, d, y, m] if d < 2 else ry[k, d - 2, x, m]
-                    pieces.append(jnp.concatenate(limbs(value), axis=0))
-                applied = partial[c, m]
-                if pieces:
-                    left = jnp.concatenate(pieces, axis=1)
-                    begin = (2 + len(near)) * wide
-                    applied = applied + fold(dot_nt(left, weights[c, m, :, begin : begin + left.shape[1]]))
+                if neighbour(c, second) is None:
+                    alone = jnp.concatenate(limbs(values(second, m)), axis=0)
+                else:
+                    alone = rows_of(k, neighbour(c, second), m)
+                plain, rolled = values(third, m), pltpu.roll(values(fourth, m), unk, 1)
+                pairs_of = (jnp.where(in_low, plain, rolled), jnp.where(in_low, rolled, plain))
+                operands = [
+                    jnp.concatenate([jnp.concatenate(limbs(both), axis=0), alone], axis=1) for both in pairs_of]
+                applied = (partial[c, m] + apply_tile(c, m, 1, operands)).T
+                applied = applied[0:rhs] + applied[rhs : 2 * rhs]
                 current = tall[k, x, y, m]
                 if k == 0:
                     following = (applied - 8.0 * current) * (1.0 / 6.0)
@@ -268,9 +285,6 @@
         total = total[0:rhs] + total[rhs : 2 * rhs]
         gram_x[k, gx] = jnp.concatenate([total, jnp.zeros((rhs, wide - count), F32)], axis=1)
 
-    for c in range(len(columns)):
-        raw_copy(c).wait()
-        prepare(c)
     axes = {"gx": (gx, n_gx, gram_x, send_gx, recv_gx), "gy": (gy, n_gy, gram_y, send_gy, recv_gy)}
 
     def gram_copy(axis, k, d, receive=False):
@@ -322,10 +336,33 @@
 
         lax.fori_loop(0, pairs // chunk, turn, 0)
 
+    gram_turn(STEPS)
+    for k in range(STEPS + 1):
+        gram_ref[k] = gram_sum("gy", k)
+
+    for k in range(STEPS + 1):
+        for axis in axes:
+            for d in range(1, axes[axis][1]):
+                gram_copy(axis, k, d).wait_send()
+    for k in range(STEPS):
+        for c in range(len(columns)):
+            for axis, side, edge in borders(c):
+                if edge:
+                    @pl.when(has(axis, side))
+                    def _():
+                        halo_copy(k, c, axis, side).wait_send()
+
+
+def factor_kernel(dims, turned, gram_ref, ortho_hbm, tri_ref, ortho, ortho_sem):
+    nx, ny, nz, unk, rhs = dims
+    columns = Columns(nx, ny).at
+    pairs, wide, cols = nz // 2, 2 * unk, (STEPS + 1) * rhs
+    chunk = chunk_of(pairs, 6)
+
     front = STEPS * rhs
     rows = lax.broadcasted_iota(jnp.int32, (front, wide), 0)
     lane = lax.broadcasted_iota(jnp.int32, (front, wide), 1)
-    lower = jnp.concatenate([gram_sum("gy", k) for k in range(STEPS)], axis=0)
+    lower = jnp.concatenate([gram_ref[k] for k in range(STEPS)], axis=0)
     square = jnp.concatenate([lower, jnp.zeros((wide - front, wide), F32)], axis=0)
     whole = jnp.where(lane > rows, square.T[0:front], lower)
     on_diagonal = jnp.where(lane == rows, whole, 0.0)
@@ -334,13 +371,11 @@
     line = lane[:1]
     whole = whole / (norm_rows * jnp.where(line < front, norm_front, 1.0))
     factored = [whole[8 * i : 8 * i + 8] for i in range(front // 8)]
-    factored = eliminate(factored, 0, rhs)
-    gram_turn(STEPS)
-    factored = eliminate(factored, rhs, front)
+    factored = eliminate(factored, 0, front)
     upper, inverse = split_factor(factored)
     inverse_full = jnp.concatenate([inverse, jnp.zeros((wide - front, wide), F32)], axis=0)
 
-    last = gram_sum("gy", STEPS)
+    last = gram_ref[STEPS]
     last_rows = lax.broadcasted_iota(jnp.int32, (rhs, wide), 0)
     last_lane = lax.broadcasted_iota(jnp.int32, (rhs, wide), 1)
     on_diagonal = jnp.where(last_lane == last_rows + front, last, 0.0)
@@ -386,17 +421,6 @@
         lax.fori_loop(0, pairs // chunk, body, 0)
         ortho_copy(c).start()
 
-    for k in range(STEPS + 1):
-        for axis in axes:
-            for d in range(1, axes[axis][1]):
-                gram_copy(axis, k, d).wait_send()
-    for k in range(STEPS):
-        for c in range(len(columns)):
-            for axis, side, edge in borders(c):
-                if edge:
-                    @pl.when(has(axis, side))
-                    def _():
-                        halo_copy(k, c, axis, side).wait_send()
     for c in range(len(columns)):
         ortho_copy(c).wait()
 
@@ -406,33 +430,37 @@
     rhs = start_block.shape[-1]
     n_gx, n_gy = lax.axis_size("gx"), lax.axis_size("gy")
     pairs, wide, cols, count = nz // 2, 2 * unk, (STEPS + 1) * rhs, nx * ny
-    assert nz % 2 == 0 and wide == 128 and rhs % 16 == 0 and cols <= wide
+    assert count > 1 and nz % 2 == 0 and wide == 128 and rhs % 16 == 0 and cols <= wide
     dma = pltpu.SemaphoreType.DMA
-    return pl.pallas_call(
-        functools.partial(kernel, (n_gx, n_gy, nx, ny, nz, unk, rhs)),
+    vmem, anywhere = pl.BlockSpec(memory_space=pltpu.VMEM), pl.BlockSpec(memory_space=pl.ANY)
+    limit = 24 * 1024 * 1024
+    local = (nx, ny, nz, unk, rhs)
+    weights = pl.pallas_call(
+        functools.partial(repack_kernel, local),
+        out_shape=jax.ShapeDtypeStruct((count, pairs, 2, 2 * unk, 4 * wide), BF16),
+        in_specs=[anywhere],
+        out_specs=vmem,
+        scratch_shapes=[pltpu.VMEM((count, nz, 7, unk, unk), F32), dma((count,))],
+        compiler_params=pltpu.CompilerParams(vmem_limit_bytes=52 * 1024 * 1024),
+        cost_estimate=pl.CostEstimate(flops=10_000_000, bytes_accessed=16_000_000, transcendentals=0),
+    )(operator_blocks)
+    turned, gram = pl.pallas_call(
+        functools.partial(steps_kernel, (n_gx, n_gy, nx, ny, nz, unk, rhs)),
         out_shape=(
-            jax.ShapeDtypeStruct((nx, ny, nz, unk, cols), F32),
-            jax.ShapeDtypeStruct((cols, cols), F32),
+            jax.ShapeDtypeStruct((count, pairs, wide, 2 * wide), BF16),
+            jax.ShapeDtypeStruct((STEPS + 1, rhs, wide), F32),
         ),
-        in_specs=[pl.BlockSpec(memory_space=pl.ANY), pl.BlockSpec(memory_space=pl.ANY)],
-        out_specs=(pl.BlockSpec(memory_space=pl.ANY), pl.BlockSpec(memory_space=pltpu.VMEM)),
+        in_specs=[vmem, vmem],
+        out_specs=(vmem, vmem),
         scratch_shapes=[
-            pltpu.VMEM((nx, ny, nz, rhs, unk), F32),
-            pltpu.VMEM((count, nz, 7, unk, unk), F32),
-            pltpu.VMEM((count, pairs, 2 * wide, 6 * wide), BF16),
             pltpu.VMEM((STEPS + 1, nx, ny, pairs, rhs, wide), F32),
             pltpu.VMEM((count, pairs, 2 * cols, wide), BF16),
-            pltpu.VMEM((count, pairs + 2, 2 * rhs, wide), BF16),
-            pltpu.VMEM((count, pairs, rhs, wide), F32),
+            pltpu.VMEM((count, pairs + 2, 2, 2 * rhs, wide), BF16),
+            pltpu.VMEM((count, pairs, wide, 2 * rhs), F32),
             pltpu.VMEM((STEPS, 2, ny, pairs, rhs, wide), F32),
             pltpu.VMEM((STEPS, 2, nx, pairs, rhs, wide), F32),
             pltpu.VMEM((STEPS + 1, n_gx, rhs, wide), F32),
             pltpu.VMEM((STEPS + 1, n_gy, rhs, wide), F32),
-            pltpu.VMEM((count, pairs, wide, 2 * wide), BF16),
-            pltpu.VMEM((count, nz, unk, cols), F32),
-            dma,
-            dma((count,)),
-            dma((count,)),
             dma((STEPS, 2, ny)),
             dma((STEPS, 2, ny)),
             dma((STEPS, 2, nx)),
@@ -442,11 +470,21 @@
             dma((STEPS + 1, n_gy)),
             dma((STEPS + 1, n_gy)),
         ],
-        compiler_params=pltpu.CompilerParams(
-            collective_id=0, has_side_effects=True, vmem_limit_bytes=52 * 1024 * 1024
+        compiler_params=pltpu.CompilerParams(collective_id=0, has_side_effects=True, vmem_limit_bytes=limit),
+        cost_estimate=pl.CostEstimate(flops=6_000_000_000, bytes_accessed=16_000_000, transcendentals=0),
+    )(weights, jnp.swapaxes(start_block, -1, -2))
+    return pl.pallas_call(
+        functools.partial(factor_kernel, local),
+        out_shape=(
+            jax.ShapeDtypeStruct((nx, ny, nz, unk, cols), F32),
+            jax.ShapeDtypeStruct((cols, cols), F32),
         ),
-        cost_estimate=pl.CostEstimate(flops=6_000_000_000, bytes_accessed=16_000_000, transcendentals=0),
-    )(operator_blocks, jnp.swapaxes(start_block, -1, -2))
+        in_specs=[vmem, vmem],
+        out_specs=(anywhere, vmem),
+        scratch_shapes=[pltpu.VMEM((count, nz, unk, cols), F32), dma((count,))],
+        compiler_params=pltpu.CompilerParams(vmem_limit_bytes=limit),
+        cost_estimate=pl.CostEstimate(flops=400_000_000, bytes_accessed=4_000_000, transcendentals=0),
+    )(turned, gram)
 
 
 def solution(mesh):

time: 54.1 us -> 60.2 us (1.11)
  Pallas kernels: 50.6 us -> 56.6 us
    pallas_call x1 -> x3, Pallas kernels: 50.6 us -> 56.6 us  [the longest x1 39 us: per_device(): pl.pallas_call(functools.partial(steps_kernel, (n_gx, n_gy, nx, ny, nz, u...]
where the time goes in v2:
time: 60.2 us; the launch traced here: 60 us
  Pallas kernels  56.6 us (94%)
  local copies, waits for them, and re-layouts  2.78 us (5%)
  between operations  0.67 us (1%)
    pallas_call x1, Pallas kernels, per_device(): pl.pallas_call(functools.partial(steps_kernel, (n_gx, n_gy, nx, ny, nz, u...  39 us
    pallas_call x1, Pallas kernels, per_device(): pl.pallas_call(functools.partial(factor_kernel, local), out_shape=(jax.Sh...  9.84 us
    pallas_call x1, Pallas kernels, per_device(): pl.pallas_call(functools.partial(repack_kernel, local), out_shape=jax.Sha...  7.71 us
    unnamed x4, local copies, waits for them, and re-layouts  2.78 us

profile of v2, /device:TPU:0, one launch (start us, length us, event | category | flops | bytes accessed | tf_op | source)
XLA Modules:
  0.0 60.0 jit_solution(8953970966329141268)
XLA Ops:
  0.6 0.0 copy-start.1
  0.6 7.7 %shard_map.41.weights = bf16[4,6,2,128,512]{4,3,2,1,0:T(8,128)(2,1)} custom-call(f32[2,2,12,7,64,64]{5,4,3,2,1,0:T(8,128)} %blocks_hbm.1), custom_call_target="tpu_custom_call" | custom-call | flops 10000000 | bytes 16000000 | tf_op jit(solution)/shard_map/pallas_call | solution.py:438
  8.4 0.0 copy-done.1
  8.4 0.0 copy-start
  8.4 2.8 %copy-done = bf16[4,6,2,128,512]{4,3,2,1,0:T(8,128)(2,1)S(1)} copy-done((bf16[4,6,2,128,512]{4,3,2,1,0:T(8,128)(2,1)S(1)}, bf16[4,6,2,128,512]{4,3,2,1,0:T(8,128)(2,1)}, u32[]{:S(2)}) %copy-start) | copy-done | bytes 6291480
  11.2 39.0 %shard_map.42 = (bf16[4,6,128,256]{3,2,1,0:T(8,128)(2,1)S(1)}, f32[5,16,128]{2,1,0:T(8,128)S(1)}) custom-call(bf16[4,6,2,128,512]{4,3,2,1,0:T(8,128)(2,1)S(1)} %copy-done, f32[2,2,12,16,64]{4,3,2,1,0:T(8,128)S(1)} %bitcast.1), custom_call_target="tpu_custom_call" | custom-call | flops 6000000000 | bytes 16000000 | tf_op jit(solution)/shard_map/pallas_call | solution.py:447
  50.2 9.8 %shard_map.43 = (f32[2,2,12,64,80]{4,3,2,1,0:T(8,128)}, f32[80,80]{1,0:T(8,128)}) custom-call(bf16[4,6,128,256]{3,2,1,0:T(8,128)(2,1)S(1)} %get-tuple-element.4.turned, f32[5,16,128]{2,1,0:T(8,128)S(1)} %get-tuple-element.5.gram_ref), custom_call_target="tpu_custom_call" | custom-call | flops 400000000 | bytes 4000000 | tf_op jit(solution)/shard_map/pallas_call | solution.py:476
Async XLA Ops:
  0.6 7.7 %copy-start.1 = (f32[2,2,12,64,16]{3,4,2,1,0:T(8,128)S(1)}, f32[2,2,12,64,16]{3,4,2,1,0:T(8,128)}, u32[]{:S(2)}) copy-start(f32[2,2,12,64,16]{3,4,2,1,0:T(8,128)} %param.3) | copy-start | bytes 589828
  8.4 2.8 %copy-start = (bf16[4,6,2,128,512]{4,3,2,1,0:T(8,128)(2,1)S(1)}, bf16[4,6,2,128,512]{4,3,2,1,0:T(8,128)(2,1)}, u32[]{:S(2)}) copy-start(bf16[4,6,2,128,512]{4,3,2,1,0:T(8,128)(2,1)} %shard_map.41.weights) | copy-start | bytes 18874372

commit v3 on v2

--- a/solution.py
+++ b/solution.py
@@ -35,7 +35,6 @@
     lane = lax.broadcasted_iota(jnp.int32, blocks[0].shape, 1)
     rows = lax.broadcasted_iota(jnp.int32, blocks[0].shape, 0)
     line = lane[:1]
-    blocks = list(blocks)
     for j in range(start, stop, 2):
         first, inside = divmod(j, 8)
         row_0 = blocks[first][inside : inside + 1, :]
@@ -56,7 +55,7 @@
             if i == first:
                 update = jnp.where(rows > inside + 1, update, jnp.where(rows == inside + 1, second, block))
             blocks[i] = update
-    return blocks
+        yield
 
 
 def split_factor(blocks):
@@ -71,73 +70,42 @@
     return upper, inverse
 
 
-class Columns:
-    def __init__(self, nx, ny):
-        self.at = [(x, y) for x in range(nx) for y in range(ny)]
-        self.nx, self.ny = nx, ny
-
-    def borders(self, c):
-        x, y = self.at[c]
-        return [("gx", 0, x == 0), ("gx", 1, x == self.nx - 1), ("gy", 0, y == 0), ("gy", 1, y == self.ny - 1)]
-
-    def order(self, c):
-        marks = [edge for _, _, edge in self.borders(c)]
-        return sorted(range(4), key=lambda d: marks[d])
-
-    def neighbour(self, c, d):
-        x, y = self.at[c]
-        x, y = x + (-1, 1, 0, 0)[d], y + (0, 0, -1, 1)[d]
-        return self.at.index((x, y)) if (x, y) in self.at else None
-
-
-def repack_kernel(dims, blocks_hbm, weights, raw, raw_sem):
-    nx, ny, nz, unk, rhs = dims
-    columns = Columns(nx, ny)
-    wide = 2 * unk
-
-    def raw_copy(c):
-        x, y = columns.at[c]
-        return pltpu.make_async_copy(blocks_hbm.at[x, y], raw.at[c], raw_sem.at[c])
-
-    for c in range(len(columns.at)):
-        raw_copy(c).start()
-    for c in range(len(columns.at)):
-        raw_copy(c).wait()
-        first, second, third, fourth = (1 + d for d in columns.order(c))
-        zeros = jnp.zeros((unk, unk), F32)
-
-        def body(m, carry):
-            low, up = raw.at[c, 2 * m], raw.at[c, 2 * m + 1]
-            halves = (
-                ((low[0], low[6]), (low[first], low[5]), (low[third], low[fourth]), (low[second], zeros)),
-                ((up[5], up[0]), (up[6], up[first]), (up[fourth], up[third]), (zeros, up[second])),
-            )
-            for half, pieces in enumerate(halves):
-                for at, (left, right) in enumerate(pieces):
-                    high, rest = limbs(jnp.concatenate([left, right], axis=1))
-                    lanes = slice(at * wide, (at + 1) * wide)
-                    weights[c, m, half, 0:unk, lanes] = high
-                    weights[c, m, half, unk : 2 * unk, lanes] = rest
-            return carry
-
-        lax.fori_loop(0, nz // 2, body, 0)
-
-def steps_kernel(dims, weights, start_ref, turned, gram_ref, tall, limb, mixed, partial, rx, ry, gram_x, gram_y,
-                 send_x, recv_x, send_y, recv_y, send_gx, recv_gx, send_gy, recv_gy):
+def kernel(dims, blocks_hbm, start_ref, turned, right_ref, tri_ref, raw, weights, tall, limb, mixed,
+           partial, rx, ry, gram_x, gram_y, raw_sem, send_x, recv_x, send_y, recv_y, send_gx, recv_gx,
+           send_gy, recv_gy):
     n_gx, n_gy, nx, ny, nz, unk, rhs = dims
     pairs = nz // 2
     wide = 2 * unk
     cols = (STEPS + 1) * rhs
     gx, gy = lax.axis_index("gx"), lax.axis_index("gy")
-    geometry = Columns(nx, ny)
-    columns, borders, order, neighbour = geometry.at, geometry.borders, geometry.order, geometry.neighbour
+    columns = [(x, y) for x in range(nx) for y in range(ny)]
     chunk = chunk_of(pairs, 6)
+
+    def raw_copy(c):
+        x, y = columns[c]
+        return pltpu.make_async_copy(blocks_hbm.at[x, y], raw.at[c], raw_sem.at[c])
+
+    for c in range(len(columns)):
+        raw_copy(c).start()
 
     barrier = pltpu.get_barrier_semaphore()
     for d in range(1, n_gx):
         pl.semaphore_signal(barrier, inc=1, device_id={"gx": lax.rem(gx + d, n_gx)}, device_id_type=MESH)
     for d in range(1, n_gy):
         pl.semaphore_signal(barrier, inc=1, device_id={"gy": lax.rem(gy + d, n_gy)}, device_id_type=MESH)
+
+    def borders(c):
+        x, y = columns[c]
+        return [("gx", 0, x == 0), ("gx", 1, x == nx - 1), ("gy", 0, y == 0), ("gy", 1, y == ny - 1)]
+
+    def order(c):
+        marks = [edge for _, _, edge in borders(c)]
+        return sorted(range(4), key=lambda d: marks[d])
+
+    def neighbour(c, d):
+        x, y = columns[c]
+        x, y = x + (-1, 1, 0, 0)[d], y + (0, 0, -1, 1)[d]
+        return columns.index((x, y)) if (x, y) in columns else None
 
     def store_basis(k, c, m, value):
         x, y = columns[c]
@@ -205,6 +173,23 @@
     for c in range(len(columns)):
         send_column(0, c)
 
+    def prepare(c):
+        first, second, third, fourth = (1 + d for d in order(c))
+        zeros = jnp.zeros((unk, unk), F32)
+
+        for m in range(pairs):
+            low, up = raw.at[c, 2 * m], raw.at[c, 2 * m + 1]
+            halves = (
+                ((low[0], low[6]), (low[first], low[5]), (low[third], low[fourth]), (low[second], zeros)),
+                ((up[5], up[0]), (up[6], up[first]), (up[fourth], up[third]), (zeros, up[second])),
+            )
+            for half, pieces in enumerate(halves):
+                for at, (left, right) in enumerate(pieces):
+                    high, rest = limbs(jnp.concatenate([left, right], axis=1))
+                    lanes = slice(at * wide, (at + 1) * wide)
+                    weights[c, m, half, 0:unk, lanes] = high
+                    weights[c, m, half, unk : 2 * unk, lanes] = rest
+
     def apply_tile(c, m, tile, operands):
         results = []
         for half in range(2):
@@ -223,16 +208,12 @@
                 def _():
                     halo_wait(k, c, axis, side)
 
-    def near_part(k, c):
-        def body(i, carry):
-            for s in range(chunk):
-                m = i * chunk + s
-                own = rows_of(k, c, m)
-                operands = [jnp.concatenate([own, mixed[c, m + 1, half]], axis=1) for half in range(2)]
-                partial[c, m] = apply_tile(c, m, 0, operands)
-            return carry
-
-        lax.fori_loop(0, pairs // chunk, body, 0)
+    def near_part(k, c, beside=iter(())):
+        for m in range(pairs):
+            own = rows_of(k, c, m)
+            operands = [jnp.concatenate([own, mixed[c, m + 1, half]], axis=1) for half in range(2)]
+            partial[c, m] = apply_tile(c, m, 0, operands)
+            next(beside, None)
 
     def far_part(k, c):
         x, y = columns[c]
@@ -283,9 +264,18 @@
                 total_low += dot_nt(left, low)
         total = total_high + total_low
         total = total[0:rhs] + total[rhs : 2 * rhs]
-        gram_x[k, gx] = jnp.concatenate([total, jnp.zeros((rhs, wide - count), F32)], axis=1)
+        return total
 
     axes = {"gx": (gx, n_gx, gram_x, send_gx, recv_gx), "gy": (gy, n_gy, gram_y, send_gy, recv_gy)}
+    early = STEPS - 1
+    assert rhs * early * (early + 1) // 2 <= wide
+
+    def put_gram(part, values):
+        values = list(values)
+        used = sum(value.shape[1] for value in values)
+        if used < wide:
+            values.append(jnp.zeros((rhs, wide - used), F32))
+        gram_x[part, gx] = jnp.concatenate(values, axis=1)
 
     def gram_copy(axis, k, d, receive=False):
         here, count, slots, send, recv = axes[axis]
@@ -312,35 +302,109 @@
         gram_y[k, gy] = gram_sum("gx", k)
         gram_send("gy", k)
 
+    def lanes_from(value, begin, count):
+        return jnp.concatenate([value[:, begin : begin + count], jnp.zeros((rhs, wide - count), F32)], axis=1)
+
+    def append(known, norm, rows_value, at):
+        rows = lax.broadcasted_iota(jnp.int32, (rhs, wide), 0)
+        lane = lax.broadcasted_iota(jnp.int32, (rhs, wide), 1)
+        on_diagonal = jnp.where(lane == rows + at, rows_value, 0.0)
+        norm_rows = jnp.sqrt(jnp.sum(on_diagonal, axis=1, keepdims=True))
+        norm = jnp.where(line // rhs == at // rhs, jnp.sqrt(jnp.sum(on_diagonal, axis=0, keepdims=True)), norm)
+        scaled = rows_value / (norm_rows * norm)
+        full = jnp.concatenate([known, jnp.zeros((wide - at, wide), F32)], axis=0)
+        side = dot_full(jnp.where(lane < at, scaled, 0.0), full, NT)
+        rest = scaled[:, at : at + rhs] - dot_full(side, side, NT)
+        rest = lanes_from(rest, 0, rhs)
+        rest = [rest[8 * i : 8 * i + 8] for i in range(rhs // 8)]
+        for _ in eliminate(rest, 0, rhs):
+            pass
+        upper, inverse = split_factor(rest)
+        below = dot_full(inverse[:, 0:rhs], dot_full(side, full))
+
+        def placed(value):
+            pieces = [jnp.zeros((rhs, at), F32), value[:, 0:rhs], jnp.zeros((rhs, wide - at - rhs), F32)]
+            return jnp.concatenate([piece for piece in pieces if piece.shape[1]], axis=1)
+
+        known = jnp.concatenate([known, placed(inverse) - below], axis=0)
+        beside = jnp.concatenate(
+            [jnp.zeros((at, wide), F32), side, jnp.zeros((wide - at - rhs, wide), F32)], axis=0).T
+        return known, norm, placed(upper), beside[0:at]
+
+    front = early * rhs
+    rows = lax.broadcasted_iota(jnp.int32, (front, wide), 0)
+    lane = lax.broadcasted_iota(jnp.int32, (front, wide), 1)
+    line = lane[:1]
+
+    def first_rows():
+        total = gram_sum("gy", 0)
+        pieces, begin = [], 0
+        for k in range(early):
+            pieces.append(lanes_from(total, begin, rhs * (k + 1)))
+            begin += rhs * (k + 1)
+        lower = jnp.concatenate(pieces, axis=0)
+        square = jnp.concatenate([lower, jnp.zeros((wide - front, wide), F32)], axis=0)
+        whole = jnp.where(lane > rows, square.T[0:front], lower)
+        on_diagonal = jnp.where(lane == rows, whole, 0.0)
+        norm_rows = jnp.sqrt(jnp.sum(on_diagonal, axis=1, keepdims=True))
+        norm = jnp.where(line < front, jnp.sqrt(jnp.sum(on_diagonal, axis=0, keepdims=True)), 1.0)
+        whole = whole / (norm_rows * norm)
+        return [whole[8 * i : 8 * i + 8] for i in range(front // 8)], norm
+
+    products = [gram_rows(0)]
+    for c in range(len(columns)):
+        raw_copy(c).wait()
+        prepare(c)
+        near_part(0, c)
     for k in range(STEPS):
-        gram_rows(k)
-        gram_send("gx", k)
-        for c in range(len(columns)):
-            near_part(k, c)
-        gram_turn(k)
+        pivots = iter(())
+        if k > 0:
+            products.append(gram_rows(k))
+        if k == early - 1:
+            put_gram(0, products)
+            gram_send("gx", 0)
+        if k == early:
+            put_gram(1, products[early:])
+            gram_send("gx", 1)
+            blocks, norm = first_rows()
+            pivots = eliminate(blocks, 0, front)
+        if k > 0:
+            for c in range(len(columns)):
+                near_part(k, c, pivots)
+        for _ in pivots:
+            pass
+        if k == early - 1:
+            gram_turn(0)
         for c in range(len(columns)):
             far_part(k, c)
             if k + 1 < STEPS:
                 send_column(k + 1, c)
-    gram_rows(STEPS)
-    gram_send("gx", STEPS)
+    gram_turn(1)
+    put_gram(2, [gram_rows(STEPS)])
+    gram_send("gx", 2)
 
     for c, (x, y) in enumerate(columns):
-        def turn(i, carry):
-            for s in range(chunk):
-                m = i * chunk + s
-                pieces = [tall[k, x, y, m] for k in range(STEPS + 1)]
-                block = jnp.concatenate(pieces + [jnp.zeros((wide - cols, wide), F32)], axis=0).T
-                turned[c, m] = jnp.concatenate(limbs(block), axis=1)
-            return carry
-
-        lax.fori_loop(0, pairs // chunk, turn, 0)
-
-    gram_turn(STEPS)
-    for k in range(STEPS + 1):
-        gram_ref[k] = gram_sum("gy", k)
-
-    for k in range(STEPS + 1):
+        for m in range(pairs):
+            pieces = [tall[k, x, y, m] for k in range(STEPS + 1)]
+            block = jnp.concatenate(pieces + [jnp.zeros((wide - cols, wide), F32)], axis=0).T
+            turned[c, m] = jnp.concatenate(limbs(block), axis=1)
+
+    upper, known = split_factor(blocks)
+    fourth_rows = gram_sum("gy", 1)
+    gram_turn(2)
+    known, norm, upper_3, beside_3 = append(known, norm, fourth_rows, front)
+    known, norm, upper_4, beside_4 = append(known, norm, gram_sum("gy", 2), front + rhs)
+    triangle = jnp.concatenate([upper + beside_3, upper_3], axis=0) + beside_4
+    triangle = jnp.concatenate([triangle, upper_4], axis=0) * norm
+    tri_ref[...] = triangle
+    inverse = jnp.concatenate([known, jnp.zeros((wide - cols, wide), F32)], axis=0) / norm
+    high, low = limbs(inverse)
+    right_ref[0:wide, 0:wide] = high
+    right_ref[0:wide, wide : 2 * wide] = high
+    right_ref[wide : 2 * wide, 0:wide] = low
+    right_ref[wide : 2 * wide, wide : 2 * wide] = low
+
+    for k in range(3):
         for axis in axes:
             for d in range(1, axes[axis][1]):
                 gram_copy(axis, k, d).wait_send()
@@ -353,74 +417,23 @@
                         halo_copy(k, c, axis, side).wait_send()
 
 
-def factor_kernel(dims, turned, gram_ref, ortho_hbm, tri_ref, ortho, ortho_sem):
-    nx, ny, nz, unk, rhs = dims
-    columns = Columns(nx, ny).at
-    pairs, wide, cols = nz // 2, 2 * unk, (STEPS + 1) * rhs
-    chunk = chunk_of(pairs, 6)
-
-    front = STEPS * rhs
-    rows = lax.broadcasted_iota(jnp.int32, (front, wide), 0)
-    lane = lax.broadcasted_iota(jnp.int32, (front, wide), 1)
-    lower = jnp.concatenate([gram_ref[k] for k in range(STEPS)], axis=0)
-    square = jnp.concatenate([lower, jnp.zeros((wide - front, wide), F32)], axis=0)
-    whole = jnp.where(lane > rows, square.T[0:front], lower)
-    on_diagonal = jnp.where(lane == rows, whole, 0.0)
-    norm_rows = jnp.sqrt(jnp.sum(on_diagonal, axis=1, keepdims=True))
-    norm_front = jnp.sqrt(jnp.sum(on_diagonal, axis=0, keepdims=True))
-    line = lane[:1]
-    whole = whole / (norm_rows * jnp.where(line < front, norm_front, 1.0))
-    factored = [whole[8 * i : 8 * i + 8] for i in range(front // 8)]
-    factored = eliminate(factored, 0, front)
-    upper, inverse = split_factor(factored)
-    inverse_full = jnp.concatenate([inverse, jnp.zeros((wide - front, wide), F32)], axis=0)
-
-    last = gram_ref[STEPS]
-    last_rows = lax.broadcasted_iota(jnp.int32, (rhs, wide), 0)
-    last_lane = lax.broadcasted_iota(jnp.int32, (rhs, wide), 1)
-    on_diagonal = jnp.where(last_lane == last_rows + front, last, 0.0)
-    norm_rows = jnp.sqrt(jnp.sum(on_diagonal, axis=1, keepdims=True))
-    norm = norm_front + jnp.sqrt(jnp.sum(on_diagonal, axis=0, keepdims=True))
-    norm = jnp.where(line < cols, norm, 1.0)
-    last = last / (norm_rows * norm)
-    side = dot_full(jnp.where(last_lane < front, last, 0.0), inverse_full, NT)
-    rest = last[:, front:cols] - dot_full(side, side, NT)
-    rest = jnp.concatenate([rest, jnp.zeros((rhs, wide - rhs), F32)], axis=1)
-    rest = eliminate([rest[8 * i : 8 * i + 8] for i in range(rhs // 8)], 0, rhs)
-    rest_upper, rest_inverse = split_factor(rest)
-    below = dot_full(rest_inverse[:, 0:rhs], dot_full(side, inverse_full))
-
-    def placed(value):
-        return jnp.concatenate(
-            [jnp.zeros((rhs, front), F32), value[:, 0:rhs], jnp.zeros((rhs, wide - cols), F32)], axis=1)
-
-    beside = jnp.concatenate([jnp.zeros((front, wide), F32), side, jnp.zeros((wide - cols, wide), F32)], axis=0)
-    triangle = jnp.concatenate([upper + beside.T[0:front], placed(rest_upper)], axis=0) * norm
-    tri_ref[...] = triangle[:, 0:cols]
-    inverse = jnp.concatenate(
-        [inverse, placed(rest_inverse) - below, jnp.zeros((wide - cols, wide), F32)], axis=0) / norm
-    inverse_high, inverse_low = limbs(inverse)
-    right = jnp.concatenate(
-        [jnp.concatenate([inverse_high, inverse_high], axis=1), jnp.concatenate([inverse_low, inverse_low], axis=1)],
-        axis=0)
+def product_kernel(dims, turned, right_ref, tri_in, ortho_hbm, tri_ref, ortho, ortho_sem):
+    nx, ny, nz, unk, cols = dims
+    wide = 2 * unk
+    columns = [(x, y) for x in range(nx) for y in range(ny)]
+    tri_ref[...] = tri_in[:, 0:cols]
 
     def ortho_copy(c):
         x, y = columns[c]
         return pltpu.make_async_copy(ortho.at[c], ortho_hbm.at[x, y], ortho_sem.at[c])
 
-    for c, (x, y) in enumerate(columns):
-        def body(i, carry):
-            for s in range(chunk):
-                m = i * chunk + s
-                product = dot_nt(turned[c, m], right)
-                result = (product[:, 0:wide] + product[:, wide : 2 * wide])[:, 0:cols]
-                ortho[c, 2 * m] = result[0:unk]
-                ortho[c, 2 * m + 1] = result[unk:wide]
-            return carry
-
-        lax.fori_loop(0, pairs // chunk, body, 0)
+    for c in range(len(columns)):
+        for m in range(nz // 2):
+            product = dot_nt(turned[c, m], right_ref[...])
+            result = (product[:, 0:wide] + product[:, wide : 2 * wide])[:, 0:cols]
+            ortho[c, 2 * m] = result[0:unk]
+            ortho[c, 2 * m + 1] = result[unk:wide]
         ortho_copy(c).start()
-
     for c in range(len(columns)):
         ortho_copy(c).wait()
 
@@ -433,58 +446,53 @@
     assert count > 1 and nz % 2 == 0 and wide == 128 and rhs % 16 == 0 and cols <= wide
     dma = pltpu.SemaphoreType.DMA
     vmem, anywhere = pl.BlockSpec(memory_space=pltpu.VMEM), pl.BlockSpec(memory_space=pl.ANY)
-    limit = 24 * 1024 * 1024
-    local = (nx, ny, nz, unk, rhs)
-    weights = pl.pallas_call(
-        functools.partial(repack_kernel, local),
-        out_shape=jax.ShapeDtypeStruct((count, pairs, 2, 2 * unk, 4 * wide), BF16),
-        in_specs=[anywhere],
-        out_specs=vmem,
-        scratch_shapes=[pltpu.VMEM((count, nz, 7, unk, unk), F32), dma((count,))],
-        compiler_params=pltpu.CompilerParams(vmem_limit_bytes=52 * 1024 * 1024),
-        cost_estimate=pl.CostEstimate(flops=10_000_000, bytes_accessed=16_000_000, transcendentals=0),
-    )(operator_blocks)
-    turned, gram = pl.pallas_call(
-        functools.partial(steps_kernel, (n_gx, n_gy, nx, ny, nz, unk, rhs)),
+    turned, right, triangle = pl.pallas_call(
+        functools.partial(kernel, (n_gx, n_gy, nx, ny, nz, unk, rhs)),
         out_shape=(
             jax.ShapeDtypeStruct((count, pairs, wide, 2 * wide), BF16),
-            jax.ShapeDtypeStruct((STEPS + 1, rhs, wide), F32),
+            jax.ShapeDtypeStruct((2 * wide, 2 * wide), BF16),
+            jax.ShapeDtypeStruct((cols, wide), F32),
         ),
-        in_specs=[vmem, vmem],
-        out_specs=(vmem, vmem),
+        in_specs=[anywhere, vmem],
+        out_specs=(vmem, vmem, vmem),
         scratch_shapes=[
+            pltpu.VMEM((count, nz, 7, unk, unk), F32),
+            pltpu.VMEM((count, pairs, 2, 2 * unk, 4 * wide), BF16),
             pltpu.VMEM((STEPS + 1, nx, ny, pairs, rhs, wide), F32),
             pltpu.VMEM((count, pairs, 2 * cols, wide), BF16),
             pltpu.VMEM((count, pairs + 2, 2, 2 * rhs, wide), BF16),
             pltpu.VMEM((count, pairs, wide, 2 * rhs), F32),
             pltpu.VMEM((STEPS, 2, ny, pairs, rhs, wide), F32),
             pltpu.VMEM((STEPS, 2, nx, pairs, rhs, wide), F32),
-            pltpu.VMEM((STEPS + 1, n_gx, rhs, wide), F32),
-            pltpu.VMEM((STEPS + 1, n_gy, rhs, wide), F32),
+            pltpu.VMEM((3, n_gx, rhs, wide), F32),
+            pltpu.VMEM((3, n_gy, rhs, wide), F32),
+            dma((count,)),
             dma((STEPS, 2, ny)),
             dma((STEPS, 2, ny)),
             dma((STEPS, 2, nx)),
             dma((STEPS, 2, nx)),
-            dma((STEPS + 1, n_gx)),
-            dma((STEPS + 1, n_gx)),
-            dma((STEPS + 1, n_gy)),
-            dma((STEPS + 1, n_gy)),
+            dma((3, n_gx)),
+            dma((3, n_gx)),
+            dma((3, n_gy)),
+            dma((3, n_gy)),
         ],
-        compiler_params=pltpu.CompilerParams(collective_id=0, has_side_effects=True, vmem_limit_bytes=limit),
+        compiler_params=pltpu.CompilerParams(
+            collective_id=0, has_side_effects=True, vmem_limit_bytes=50 * 1024 * 1024
+        ),
         cost_estimate=pl.CostEstimate(flops=6_000_000_000, bytes_accessed=16_000_000, transcendentals=0),
-    )(weights, jnp.swapaxes(start_block, -1, -2))
+    )(operator_blocks, jnp.swapaxes(start_block, -1, -2))
     return pl.pallas_call(
-        functools.partial(factor_kernel, local),
+        functools.partial(product_kernel, (nx, ny, nz, unk, cols)),
         out_shape=(
             jax.ShapeDtypeStruct((nx, ny, nz, unk, cols), F32),
             jax.ShapeDtypeStruct((cols, cols), F32),
         ),
-        in_specs=[vmem, vmem],
+        in_specs=[vmem, vmem, vmem],
         out_specs=(anywhere, vmem),
         scratch_shapes=[pltpu.VMEM((count, nz, unk, cols), F32), dma((count,))],
-        compiler_params=pltpu.CompilerParams(vmem_limit_bytes=limit),
+        compiler_params=pltpu.CompilerParams(vmem_limit_bytes=24 * 1024 * 1024),
         cost_estimate=pl.CostEstimate(flops=400_000_000, bytes_accessed=4_000_000, transcendentals=0),
-    )(turned, gram)
+    )(turned, right, triangle)
 
 
 def solution(mesh):

time: 60.2 us -> 45.2 us (0.75)
  Pallas kernels: 56.6 us -> 43.4 us
  local copies, waits for them, and re-layouts: 2.78 us -> 0.99 us
    pallas_call x3 -> x2, Pallas kernels: 56.6 us -> 43.4 us  [the longest x1 40.9 us: per_device(): pl.pallas_call(functools.partial(kernel, (n_gx, n_gy, nx, ny, nz, unk, rh...]
    unnamed x4 -> x2, local copies, waits for them, and re-layouts: 2.78 us -> 0.99 us
where the time goes in v3:
time: 45.2 us; the launch traced here: 45 us
  Pallas kernels  43.4 us (96%)
  local copies, waits for them, and re-layouts  0.99 us (2%)
  between operations  0.65 us (1%)
    pallas_call x1, Pallas kernels, per_device(): pl.pallas_call(functools.partial(kernel, (n_gx, n_gy, nx, ny, nz, unk, rh...  40.9 us
    pallas_call x1, Pallas kernels, per_device(): pl.pallas_call(functools.partial(product_kernel, (nx, ny, nz, unk, cols))...  2.51 us
    unnamed x2, local copies, waits for them, and re-layouts  0.99 us

profile of v3, /device:TPU:0, one launch (start us, length us, event | category | flops | bytes accessed | tf_op | source)
XLA Modules:
  0.0 45.0 jit_solution(17431504128922971850)
XLA Ops:
  0.6 0.0 copy-start
  0.6 1.0 %copy-done = f32[2,2,12,64,16]{3,4,2,1,0:T(8,128)S(1)} copy-done((f32[2,2,12,64,16]{3,4,2,1,0:T(8,128)S(1)}, f32[2,2,12,64,16]{3,4,2,1,0:T(8,128)}, u32[]{:S(2)}) %copy-start) | copy-done | bytes 196632
  1.6 40.9 %shard_map.41 = (bf16[4,6,128,256]{3,2,1,0:T(8,128)(2,1)S(1)}, bf16[256,256]{1,0:T(8,128)(2,1)S(1)}, f32[80,128]{1,0:T(8,128)S(1)}) custom-call(f32[2,2,12,7,64,64]{5,4,3,2,1,0:T(8,128)} %blocks_hbm.1, f32[2,2,12,16,64]{4,3,2,1,0:T(8,128)S(1)} %bitcast.1), custom_call_target="tpu_custom_call" | custom-call | flops 6000000000 | bytes 16000000 | tf_op jit(solution)/shard_map/pallas_call | solution.py:449
  42.5 2.5 %shard_map.42 = (f32[2,2,12,64,80]{4,3,2,1,0:T(8,128)}, f32[80,80]{1,0:T(8,128)}) custom-call(bf16[4,6,128,256]{3,2,1,0:T(8,128)(2,1)S(1)} %get-tuple-element.5.turned, bf16[256,256]{1,0:T(8,128)(2,1)S(1)} %get-tuple-element.6.right_ref, f32[80,128]{1,0:T(8,128)S(1)} %get-tuple-element.7.tri_in), custom_call_target="tpu_custom_call" | custom-call | flops 400000000 | bytes 4000000 | tf_op jit(solution)/shard_map/pallas_call | solution.py:484
Async XLA Ops:
  0.6 1.0 %copy-start = (f32[2,2,12,64,16]{3,4,2,1,0:T(8,128)S(1)}, f32[2,2,12,64,16]{3,4,2,1,0:T(8,128)}, u32[]{:S(2)}) copy-start(f32[2,2,12,64,16]{3,4,2,1,0:T(8,128)} %param.3) | copy-start | bytes 589828

commit v4 on v3

--- a/solution.py
+++ b/solution.py
@@ -250,21 +250,20 @@
 
         lax.fori_loop(0, pairs // chunk, body, 0)
 
-    def gram_rows(k):
-        count = rhs * (k + 1)
-        total_high = jnp.zeros((2 * rhs, count), F32)
-        total_low = jnp.zeros((2 * rhs, count), F32)
+    def gram_rows(begin, end):
+        count, size = rhs * end, rhs * (end - begin)
+        total_high = jnp.zeros((2 * size, count), F32)
+        total_low = jnp.zeros((2 * size, count), F32)
         for c in range(len(columns)):
             for m in range(0, pairs, 2):
                 span = range(m, min(m + 2, pairs))
-                left = jnp.concatenate([rows_of(k, c, q) for q in span], axis=1)
                 high = jnp.concatenate([limb[c, q, 0:count] for q in span], axis=1)
                 low = jnp.concatenate([limb[c, q, cols : cols + count] for q in span], axis=1)
+                left = jnp.concatenate([high[count - size :], low[count - size :]], axis=0)
                 total_high += dot_nt(left, high)
                 total_low += dot_nt(left, low)
         total = total_high + total_low
-        total = total[0:rhs] + total[rhs : 2 * rhs]
-        return total
+        return total[0:size] + total[size : 2 * size]
 
     axes = {"gx": (gx, n_gx, gram_x, send_gx, recv_gx), "gy": (gy, n_gy, gram_y, send_gy, recv_gy)}
     early = STEPS - 1
@@ -351,20 +350,18 @@
         whole = whole / (norm_rows * norm)
         return [whole[8 * i : 8 * i + 8] for i in range(front // 8)], norm
 
-    products = [gram_rows(0)]
     for c in range(len(columns)):
         raw_copy(c).wait()
         prepare(c)
         near_part(0, c)
     for k in range(STEPS):
         pivots = iter(())
-        if k > 0:
-            products.append(gram_rows(k))
         if k == early - 1:
-            put_gram(0, products)
+            products = gram_rows(0, early)
+            put_gram(0, [products[rhs * i : rhs * (i + 1), 0 : rhs * (i + 1)] for i in range(early)])
             gram_send("gx", 0)
         if k == early:
-            put_gram(1, products[early:])
+            put_gram(1, [gram_rows(early, STEPS)])
             gram_send("gx", 1)
             blocks, norm = first_rows()
             pivots = eliminate(blocks, 0, front)
@@ -380,7 +377,7 @@
             if k + 1 < STEPS:
                 send_column(k + 1, c)
     gram_turn(1)
-    put_gram(2, [gram_rows(STEPS)])
+    put_gram(2, [gram_rows(STEPS, STEPS + 1)])
     gram_send("gx", 2)
 
     for c, (x, y) in enumerate(columns):

time: 45.2 us -> 45.4 us (level)
  no operation moved by 1% of the time
where the time goes in v4:
time: 45.4 us; the launch traced here: 45.2 us
  Pallas kernels  43.6 us (96%)
  local copies, waits for them, and re-layouts  0.99 us (2%)
  between operations  0.65 us (1%)
    pallas_call x1, Pallas kernels, per_device(): pl.pallas_call(functools.partial(kernel, (n_gx, n_gy, nx, ny, nz, unk, rh...  41.1 us
    pallas_call x1, Pallas kernels, per_device(): pl.pallas_call(functools.partial(product_kernel, (nx, ny, nz, unk, cols))...  2.51 us
    unnamed x2, local copies, waits for them, and re-layouts  0.99 us

profile of v4, /device:TPU:0, one launch (start us, length us, event | category | flops | bytes accessed | tf_op | source)
XLA Modules:
  0.0 45.2 jit_solution(11311920461840295340)
XLA Ops:
  0.6 0.0 copy-start
  0.6 1.0 %copy-done = f32[2,2,12,64,16]{3,4,2,1,0:T(8,128)S(1)} copy-done((f32[2,2,12,64,16]{3,4,2,1,0:T(8,128)S(1)}, f32[2,2,12,64,16]{3,4,2,1,0:T(8,128)}, u32[]{:S(2)}) %copy-start) | copy-done | bytes 196632
  1.6 41.1 %shard_map.41 = (bf16[4,6,128,256]{3,2,1,0:T(8,128)(2,1)S(1)}, bf16[256,256]{1,0:T(8,128)(2,1)S(1)}, f32[80,128]{1,0:T(8,128)S(1)}) custom-call(f32[2,2,12,7,64,64]{5,4,3,2,1,0:T(8,128)} %blocks_hbm.1, f32[2,2,12,16,64]{4,3,2,1,0:T(8,128)S(1)} %bitcast.1), custom_call_target="tpu_custom_call" | custom-call | flops 6000000000 | bytes 16000000 | tf_op jit(solution)/shard_map/pallas_call | solution.py:446
  42.7 2.5 %shard_map.42 = (f32[2,2,12,64,80]{4,3,2,1,0:T(8,128)}, f32[80,80]{1,0:T(8,128)}) custom-call(bf16[4,6,128,256]{3,2,1,0:T(8,128)(2,1)S(1)} %get-tuple-element.5.turned, bf16[256,256]{1,0:T(8,128)(2,1)S(1)} %get-tuple-element.6.right_ref, f32[80,128]{1,0:T(8,128)S(1)} %get-tuple-element.7.tri_in), custom_call_target="tpu_custom_call" | custom-call | flops 400000000 | bytes 4000000 | tf_op jit(solution)/shard_map/pallas_call | solution.py:481
Async XLA Ops:
  0.6 1.0 %copy-start = (f32[2,2,12,64,16]{3,4,2,1,0:T(8,128)S(1)}, f32[2,2,12,64,16]{3,4,2,1,0:T(8,128)}, u32[]{:S(2)}) copy-start(f32[2,2,12,64,16]{3,4,2,1,0:T(8,128)} %param.3) | copy-start | bytes 589828
